TPU v7x, 256 devices: a whole 4x4x8 slice. The times are simulated.
256 devices in a mesh: sector: 16 (over y, x), mode: 16 (over z, core).
Axes of the slice: x: 4, y: 4, z: 8, core: 2. Of those that a mesh axis runs over, the one named last changes fastest.
Arguments:
- pressure: bfloat16 [64, 256, 16384], P('sector', None, 'mode'), may hold values from -6 to 6
- basis: bfloat16 [16384, 1024], P('mode'), may hold values from -0.0625 to 0.0625
- recovery: bfloat16 [1024, 16384], P(None, 'mode'), may hold values from -0.1875 to 0.1875
- omega: float32 [33, 1024], P(None, 'mode'), may hold values from 0.5 to 4
- damping: float32 [33, 1024], P(None, 'mode'), may hold values from 0.1 to 0.4
- harmonic: int32 [256], replicated, may hold values from 1 to 16
Outputs:
- stress_re: bfloat16 [64, 256, 16384], P('sector', None, 'mode')
- stress_im: bfloat16 [64, 256, 16384], P('sector', None, 'mode')
All inputs are finite; a program needn't handle non-finite values.
Results may differ from a plain program's by a relative error of at most 0.027.
Values may be sent and summed in bfloat16 or wider, within the bound.
A program may use at most 64 MiB of HBM per device.

v0:
```python
import math

import jax
import jax.numpy as jnp
from jax import lax
from jax.sharding import PartitionSpec as P


def phase_tables(sector_count):
    wave_index = jnp.arange(sector_count, dtype=jnp.int32)
    phases = wave_index[:, None] * wave_index[None, :] % sector_count
    angles = 2.0 * math.pi / sector_count * phases.astype(jnp.float32)
    return (jnp.cos(angles), jnp.sin(angles))


def solve_owned(forces, freq_block, damp_block, harmonic):
    high = lax.Precision.HIGHEST
    sector_count = forces.shape[1]
    cos_table, sine_table = phase_tables(sector_count)
    force_data = forces.astype(jnp.float32)
    spec_re = jnp.einsum("ks,mst->mkt", cos_table, force_data, precision=high)
    spec_im = -jnp.einsum("ks,mst->mkt", sine_table, force_data, precision=high)
    freq_wave = jnp.concatenate([freq_block, freq_block[-2:0:-1]], 0).T[:, :, None]
    damp_wave = jnp.concatenate([damp_block, damp_block[-2:0:-1]], 0).T[:, :, None]
    drive = (0.25 * harmonic.astype(jnp.float32))[None, None, :]
    stiff_part = freq_wave * freq_wave - drive * drive
    loss_part = 2.0 * damp_wave * freq_wave * drive
    magnitude = stiff_part * stiff_part + loss_part * loss_part
    recv_re = stiff_part / magnitude
    recv_im = -loss_part / magnitude
    resp_re = recv_re * spec_re - recv_im * spec_im
    resp_im = recv_re * spec_im + recv_im * spec_re
    back_re = (
        jnp.einsum("ks,mkt->mst", cos_table, resp_re, precision=high)
        - jnp.einsum("ks,mkt->mst", sine_table, resp_im, precision=high)
    ) / sector_count
    back_im = (
        jnp.einsum("ks,mkt->mst", sine_table, resp_re, precision=high)
        + jnp.einsum("ks,mkt->mst", cos_table, resp_im, precision=high)
    ) / sector_count
    return jnp.stack([back_re, back_im], 1).astype(jnp.bfloat16)


def local(pressure, basis, recovery, omega, damping, harmonic):
    sector_local, samples, node_local = pressure.shape
    modes_all = basis.shape[1]
    mode_local = modes_all // lax.axis_size("mode")
    pressure_rows = pressure.reshape(sector_local * samples, node_local)
    loads = lax.psum_scatter(
        lax.dot_general(
            basis, pressure_rows, (((0,), (1,)), ((), ())), preferred_element_type=jnp.float32
        ).astype(jnp.bfloat16),
        "mode",
        scatter_dimension=0,
        tiled=True,
    )
    forces = loads.reshape(mode_local, sector_local, samples)
    at_owners = lax.all_to_all(forces, "sector", split_axis=0, concat_axis=1, tiled=True)
    owner_count = at_owners.shape[0]
    first_mode = lax.axis_index("sector") * owner_count
    freq_block = lax.dynamic_slice_in_dim(omega, first_mode, owner_count, 1)
    damp_block = lax.dynamic_slice_in_dim(damping, first_mode, owner_count, 1)
    responses = solve_owned(at_owners, freq_block, damp_block, harmonic)
    width_out = recovery.shape[1]
    in_sectors = lax.all_to_all(responses, "sector", split_axis=2, concat_axis=0, tiled=True)
    piece = lax.all_gather(in_sectors, "mode", axis=0, tiled=True)
    stress = lax.dot_general(
        piece.reshape(piece.shape[0], -1),
        recovery,
        (((0,), (0,)), ((), ())),
        preferred_element_type=jnp.float32,
    )
    stress = stress.reshape(2, sector_local, samples, width_out)
    return (stress[0].astype(jnp.bfloat16), stress[1].astype(jnp.bfloat16))


def solution(mesh):
    in_specs = (
        P("sector", None, "mode"),
        P("mode", None),
        P(None, "mode"),
        P(None, "mode"),
        P(None, "mode"),
        P(),
    )
    out_specs = (P("sector", None, "mode"), P("sector", None, "mode"))
    return jax.shard_map(local, mesh=mesh, in_specs=in_specs, out_specs=out_specs, check_vma=False)
```

profile of v0, /device:TPU:1, one launch (start us, length us, event | category | flops | bytes accessed | tf_op | source)
XLA Modules:
  0.0 171.8 jit_solution(12009478216596476153)
XLA Ops:
  7.2 0.0 copy-start
  7.2 0.0 reduce-scatter.2.cloned.1.call-start
  7.2 1.5 copy-done
  8.8 5.3 %convolution_convert_fusion.1 = bf16[1024,1024]{1,0:T(8,128)(2,1)} fusion(bf16[1024,1024]{1,0:T(8,128)(2,1)} %param.7, bf16[1024,1024]{1,0:T(8,128)(2,1)S(1)} %bitcast.55), kind=kOutput, calls=%fused_computation.1 | convolution fusion | flops 2148532224 | bytes 6291456 | tf_op jit(solution)/shard_map/dot_general | solution.py:50
  14.1 0.0 copy-start.3
  14.1 0.0 copy-start.1
  14.1 0.0 copy-start.2
  14.1 0.0 reduce-scatter.2.cloned.1.call-update
  14.1 0.6 copy-done.3
  14.7 59.6 %reduce-scatter.2.cloned.1.call-done = bf16[64,1024]{1,0:T(8,128)(2,1)} async-done(((bf16[1024,1024]{1,0:T(8,128)(2,1)}), bf16[64,1024]{1,0:T(8,128)(2,1)}) %reduce-scatter.2.cloned.1.call-update) | async-done | bytes 131088 | tf_op jit(solution)/shard_map/reduce_scatter | solution.py:49
  74.4 1.6 reshape.29
  76.0 6.5 %all-to-all-start = ((bf16[64,4,256]{2,1,0:T(4,128)(2,1)}), bf16[64,4,256]{2,1,0:T(4,128)(2,1)S(1)}, u32[]{:S(2)}, u32[]{:S(2)}) async-start(bf16[64,4,256]{2,1,0:T(4,128)(2,1)} %reshape.29), calls=%async_computation.1 | async-start | bytes 262144 | tf_op jit(solution)/shard_map/all_to_all | solution.py:58
  82.5 0.0 all-gather.2.cloned.1.call-start
  82.6 0.0 copy-done.1
  82.6 0.0 copy-done.2
  82.6 0.1 constant_dynamic-slice_fusion
  82.7 0.1 copy.31
  82.8 0.1 copy.30
  82.9 0.1 slice.16
  82.9 0.1 rev.6
  83.0 0.1 slice.17
  83.1 0.1 rev.7
  83.2 0.1 multiply_bitcast_fusion
  83.3 6.1 %all-to-all-done = bf16[64,4,256]{2,1,0:T(4,128)(2,1)S(1)} async-done(((bf16[64,4,256]{2,1,0:T(4,128)(2,1)}), bf16[64,4,256]{2,1,0:T(4,128)(2,1)S(1)}, u32[]{:S(2)}, u32[]{:S(2)}) %all-to-all-start) | async-done | bytes 131104 | tf_op jit(solution)/shard_map/all_to_all | solution.py:58
  89.5 0.4 fusion.2
  89.9 0.5 multiply_add_fusion
  90.4 0.5 fusion.12
  91.0 0.5 fusion.17
  91.5 0.5 fusion.5
  92.0 0.5 fusion.6
  92.6 0.2 copy.24
  92.8 10.3 %all_to_all.36 = bf16[4,2,64,256]{3,0,1,2:T(4,128)(2,1)S(1)} all-to-all(bf16[4,2,64,256]{3,0,1,2:T(4,128)(2,1)S(1)} %copy.24), channel_id=1, replica_groups=mesh['sector'=16,'mode'=16] {'sector'}, dimensions={2} | all-to-all | bytes 524288 | tf_op jit(solution)/shard_map/all_to_all | solution.py:65
  103.2 0.8 copy.25
  104.0 0.0 all-gather.2.cloned.1.call-update
  104.0 43.3 %all-gather.2.cloned.1.call-done = bf16[1024,2,4,256]{3,2,1,0:T(4,128)(2,1)} async-done(((bf16[64,2,4,256]{3,2,1,0:T(4,128)(2,1)}), bf16[1024,2,4,256]{3,2,1,0:T(4,128)(2,1)}) %all-gather.2.cloned.1.call-update) | async-done | bytes 4194320 | tf_op jit(solution)/shard_map/all_gather | solution.py:66
  147.3 7.8 %reshape.30 = bf16[1024,2048]{1,0:T(8,128)(2,1)} reshape(bf16[1024,2,4,256]{3,2,1,0:T(4,128)(2,1)} %all-gather.2.cloned.1.call-done) | data formatting | bytes 8388608 | tf_op jit(solution)/shard_map/reshape | solution.py:68
  155.1 7.4 %convolution_convert_fusion = bf16[2048,1024]{1,0:T(8,128)(2,1)S(1)} fusion(bf16[1024,2048]{1,0:T(8,128)(2,1)} %reshape.30, bf16[1024,1024]{1,0:T(8,128)(2,1)} %param.8), kind=kOutput, calls=%fused_computation | convolution fusion | flops 4297064448 | bytes 10485760 | tf_op jit(solution)/shard_map/dot_general | solution.py:67
  162.6 2.4 %fusion.58 = (bf16[1024,1024]{1,0:T(8,128)(2,1)}, bf16[1024,1024]{1,0:T(8,128)(2,1)}) fusion(bf16[2048,1024]{1,0:T(8,128)(2,1)S(1)} %convolution_convert_fusion), kind=kLoop, calls=%fused_computation.75 | loop fusion | bytes 8388608 | tf_op jit(solution)/shard_map/slice | solution.py:74
  (4 shorter events, 0.1 us)
Async XLA Ops:
  7.2 1.6 copy-start
  7.2 67.2 %reduce-scatter.2.cloned.1.call-start = ((), (), s32[]{:S(2)}) async-start(), calls=%async_computation.3 | async-start | bytes 2228224 | tf_op jit(solution)/shard_map/reduce_scatter | solution.py:49
  14.1 0.7 copy-start.3
  14.1 68.5 %copy-start.1 = (f32[33,64]{1,0:T(8,128)S(1)}, f32[33,64]{1,0:T(8,128)}, u32[]{:S(2)}) copy-start(f32[33,64]{1,0:T(8,128)} %param.10) | copy-start | bytes 25348
  14.1 68.5 %copy-start.2 = (f32[33,64]{1,0:T(8,128)S(1)}, f32[33,64]{1,0:T(8,128)}, u32[]{:S(2)}) copy-start(f32[33,64]{1,0:T(8,128)} %param.9) | copy-start | bytes 25348
  76.0 13.4 %all-to-all-start = ((bf16[64,4,256]{2,1,0:T(4,128)(2,1)}), bf16[64,4,256]{2,1,0:T(4,128)(2,1)S(1)}, u32[]{:S(2)}, u32[]{:S(2)}) async-start(bf16[64,4,256]{2,1,0:T(4,128)(2,1)} %reshape.29), calls=%async_computation.1 | async-start | bytes 262144 | tf_op jit(solution)/shard_map/all_to_all | solution.py:58
  82.5 64.8 %all-gather.2.cloned.1.call-start = ((), (), s32[]{:S(2)}) async-start(), calls=%async_computation.4 | async-start | bytes 4456448 | tf_op jit(solution)/shard_map/all_gather | solution.py:66
Sparse Core Ops, SparseCore 0:
  14.2 60.1 reduce-scatter.1
  104.1 43.1 all-gather.1
where the time goes:
time: 172 us
  waiting for transfers between devices  109 us (63%)
  local copies, waits for them, and re-layouts  15.8 us (9%)
  matrix products  15.8 us (9%)
  between operations  14.2 us (8%)
  blocking collectives  10.3 us (6%)
  starting transfers between devices  6.6 us (4%)
    reduce_scatter x1, waiting for transfers between devices, local(): lax.psum_scatter(lax.dot_general(basis, pressure_rows, (((0,), (1,)), (()...  59.6 us
    all_gather x1, waiting for transfers between devices, local(): piece = lax.all_gather(in_sectors, 'mode', axis=0, tiled=True)  43.3 us
    all_to_all x1, blocking collectives, local(): lax.all_to_all(responses, 'sector', split_axis=2, concat_axis=0, tiled=True)  10.3 us
    reshape x1, local copies, waits for them, and re-layouts, local(): piece.reshape(piece.shape[0], -1)  7.78 us
    dot_general x1, matrix products, local(): lax.dot_general(piece.reshape(piece.shape[0], -1), recovery, (((0,), (0,)...  7.43 us
    all_to_all x1, starting transfers between devices, local(): lax.all_to_all(forces, 'sector', split_axis=0, concat_axis=1, tiled=True)  6.52 us
    all_to_all x1, waiting for transfers between devices, local(): lax.all_to_all(forces, 'sector', split_axis=0, concat_axis=1, tiled=True)  6.1 us
    dot_general x1, matrix products, local(): lax.dot_general(basis, pressure_rows, (((0,), (1,)), ((), ())), preferred...  5.29 us
  transfers between devices with their start and end apart: 3, of which 3 were waited for; matrix products, arithmetic and copies ran while one was open for 0% of the time, Pallas kernels for 0%

commit v1 on v0

v1 whole, which is shorter than its diff:
```python
import functools
import math

import jax
import jax.numpy as jnp
import numpy as np
from jax import lax
from jax.experimental import pallas as pl
from jax.experimental.pallas import tpu as pltpu
from jax.sharding import PartitionSpec as P

MESH = pl.DeviceIdType.MESH
SECTORS = 64
COLS = 16
LANES = 128
GROUP = 8
CHUNKS = 4
F32 = jnp.float32
BF16 = jnp.bfloat16


def transforms():
    waves = np.arange(SECTORS)
    half = SECTORS // 2
    angle = 2.0 * np.pi / SECTORS * ((waves[:, None] * waves[None, :]) % SECTORS)
    forward = np.concatenate([np.cos(angle[: half + 1]), -np.sin(angle[1:half])], 0)
    weight = np.full((SECTORS,), 2.0 / SECTORS)
    weight[0] = weight[half] = 1.0 / SECTORS
    inverse = forward.T * weight[None, :]
    eye = np.eye(GROUP)
    return (
        np.kron(forward, eye).astype(jnp.bfloat16),
        np.kron(inverse, eye).astype(jnp.bfloat16),
    )


def kernel(
    press_hbm, basis_hbm, rec_hbm, omega_hbm, damp_hbm, harm_hbm, fwd_hbm, inv_hbm,
    out_re, out_im,
    press, basis, rec, omega, damp, harm, fwd, inv,
    own, give, take, params, params_in, recv_re, recv_im,
    ring_out, ring_in, loads_out, loads_in, resp_out, gathered, total,
    stage_re, stage_im,
    load_sem, give_s, give_r, par_sem, ring_s, ring_r, fwd_s, fwd_r, back_s, back_r,
    ag_s, ag_r, pair_s, pair_r, out_sem,
):
    col = lax.axis_index("sector")
    place = lax.axis_index("mode")
    z = place // 2
    core = place % 2
    other = 1 - core
    y = col // 4
    partner = (col, z * 2 + other)

    def at_z(step):
        return (z + step + 8) % 8

    up = (col, at_z(1) * 2 + core)
    down = (col, at_z(-1) * 2 + core)
    beside = (up, down)

    loads = [
        pltpu.make_async_copy(a, b, load_sem.at[n])
        for n, (a, b) in enumerate(
            (
                (press_hbm, press), (basis_hbm, basis), (omega_hbm, omega),
                (damp_hbm, damp), (harm_hbm, harm), (fwd_hbm, fwd), (inv_hbm, inv),
                (rec_hbm, rec),
            )
        )
    ]
    for copy in loads:
        copy.start()

    barrier = pltpu.get_barrier_semaphore()
    for device in (up, down, partner):
        pl.semaphore_signal(barrier, inc=1, device_id=device, device_id_type=MESH)
    for step in range(1, COLS):
        pl.semaphore_signal(
            barrier, inc=1, device_id=((col + step) % COLS, place), device_id_type=MESH
        )

    loads[0].wait()
    loads[1].wait()

    def partial(half, target):
        rows = press[:, pl.ds(pl.multiple_of(half * 128, 128), 128), :].reshape(512, 1024)

        def tile(n, _):
            part = jnp.dot(
                rows,
                basis[:, pl.ds(pl.multiple_of(n * 256, 256), 256)],
                preferred_element_type=F32,
            ).astype(target.dtype)
            for b in range(2):
                for q in range(CHUNKS):
                    for s in range(4):
                        target[2 * n + b, q, s * 32 : s * 32 + 32, :] = part[
                            s * 128 + q * 32 : s * 128 + q * 32 + 32, b * 128 : b * 128 + 128
                        ]
            return 0

        lax.fori_loop(0, 4, tile, 0)

    partial(other, give)
    partial(core, own)

    loads[2].wait()
    loads[3].wait()
    loads[4].wait()
    params[...] = jnp.zeros_like(params)
    for n, ref in enumerate((omega, damp)):
        mine = ref[...]
        none = jnp.zeros_like(mine)
        params[n, 0:33, :] = jnp.concatenate(
            [jnp.where(core == 0, mine, none), jnp.where(core == 1, mine, none)], 1
        )

    pl.semaphore_wait(barrier, COLS + 2)

    def pair_copy(n, block):
        return pltpu.make_async_remote_copy(
            src_ref=give.at[block], dst_ref=take.at[block], send_sem=give_s.at[n],
            recv_sem=give_r.at[n], device_id=partner, device_id_type=MESH,
        )

    order = (4, 3, -3, 2, -2, 1, -1, 0)
    pair_copies = {}
    for n, step in enumerate(order):
        pair_copies[step] = pair_copy(n, at_z(step))
        pair_copies[step].start()
    par_copy = pltpu.make_async_remote_copy(
        src_ref=params, dst_ref=params_in, send_sem=par_sem.at[0], recv_sem=par_sem.at[1],
        device_id=partner, device_id_type=MESH,
    )
    par_copy.start()

    def ring_copy(way, hop, q):
        return pltpu.make_async_remote_copy(
            src_ref=ring_out.at[way, hop, q], dst_ref=ring_in.at[way, hop, q],
            send_sem=ring_s.at[way, hop, q], recv_sem=ring_r.at[way, hop, q],
            device_id=beside[way], device_id_type=MESH,
        )

    def ring_step(way, hop, q, add):
        block = at_z((4 - hop) * (1, -1)[way])
        value = own[block, q] + take[block, q].astype(F32)
        if add:
            ring_copy(way, hop - 1, q).wait_recv()
            value = value + ring_in[way, hop - 1, q].astype(F32)
        ring_out[way, hop, q] = value.astype(BF16)
        ring_copy(way, hop, q).start()

    longer = ((0, 1), (2, 3))
    shorter = ((2, 3), (0, 1))
    pair_copies[4].wait_recv()
    for n in range(2):
        for way in range(2):
            ring_step(way, 0, longer[way][n], False)
    for hop in range(1, 4):
        pair_copies[4 - hop].wait_recv()
        pair_copies[hop - 4].wait_recv()
        for n in range(2):
            for way in range(2):
                ring_step(way, hop, shorter[way][n], hop > 1)
        for n in range(2):
            for way in range(2):
                ring_step(way, hop, longer[way][n], True)
        if hop == 1:
            par_copy.wait_recv()
            both = params[...] + params_in[...]
            freq = both[0, 0:33, :][:, None, :]
            ratio = both[1, 0:33, :][:, None, :]
            sample = lax.broadcasted_iota(jnp.int32, (GROUP, 256), 0)
            lane = lax.broadcasted_iota(jnp.int32, (GROUP, 256), 1)
            here = lane == core * 128 + col * GROUP + sample
            picked = jnp.where(here, harm[...].astype(F32), 0.0)
            drive = (0.25 * jnp.sum(picked, axis=1, keepdims=True))[None, :, :]
            stiff = freq * freq - drive * drive
            loss = 2.0 * ratio * freq * drive
            size = stiff * stiff + loss * loss
            for ref, value in ((recv_re, stiff / size), (recv_im, -loss / size)):
                ref[0:33] = value
                ref[33:64] = value[1:32]

    def fwd_copy(to, source):
        return pltpu.make_async_remote_copy(
            src_ref=loads_out.at[to], dst_ref=loads_in.at[source], send_sem=fwd_s.at[to],
            recv_sem=fwd_r.at[source], device_id=(to, place), device_id_type=MESH,
        )

    pair_copies[0].wait_recv()
    for q in range(CHUNKS):
        for way in range(2):
            ring_copy(way, 3, q).wait_recv()
        force = (
            own[z, q] + take[z, q].astype(F32)
            + ring_in[0, 3, q].astype(F32) + ring_in[1, 3, q].astype(F32)
        )
        for o in range(4):
            to = q * 4 + o
            for pair in range(2):
                at = 2 * pair * 32 + o * 8
                loads_out[to, pair] = jnp.concatenate(
                    [force[at : at + 8], force[at + 32 : at + 40]], 0
                ).astype(BF16)

            @pl.when(to != col)
            def _():
                fwd_copy(to, col).start()

    loads_in[col] = loads_out[col]

    loads[5].wait()
    loads[6].wait()
    for source in range(COLS):

        @pl.when(source != col)
        def _():
            fwd_copy(source, source).wait_recv()

    wave = jnp.dot(fwd[...], loads_in[...].reshape(512, LANES), preferred_element_type=F32)
    response = jnp.concatenate(
        [
            (wave * recv_re[...].reshape(512, LANES)).astype(BF16),
            (wave * recv_im[...].reshape(512, LANES)).astype(BF16),
        ],
        1,
    )
    back = jnp.dot(inv[...], response, preferred_element_type=F32)
    resp_out[...] = jnp.concatenate(
        [
            back[:, :LANES].reshape(SECTORS, GROUP, LANES),
            back[:, LANES:].reshape(SECTORS, GROUP, LANES),
        ],
        1,
    ).astype(BF16)

    def back_copy(to, source):
        return pltpu.make_async_remote_copy(
            src_ref=resp_out.at[pl.ds(to * 4, 4)],
            dst_ref=gathered.at[z, core, source // 4, source % 4],
            send_sem=back_s.at[to], recv_sem=back_r.at[source],
            device_id=(to, place), device_id_type=MESH,
        )

    for step in (10, 9, 11, 6, 14, 5, 7, 13, 15, 2, 8, 1, 3, 4, 12):
        back_copy((col + step) % COLS, col).start()
    gathered[z, core, y, col % 4] = resp_out[pl.ds(col * 4, 4)]

    def ag_copy(way, hop, q):
        block = at_z((1 - hop) * (1, -1)[way])
        return pltpu.make_async_remote_copy(
            src_ref=gathered.at[block, core, q], dst_ref=gathered.at[block, core, q],
            send_sem=ag_s.at[way, hop - 1, q], recv_sem=ag_r.at[way, hop - 1, q],
            device_id=beside[way], device_id_type=MESH,
        )

    def ag_arrival(way, hop, q):
        block = at_z(hop * (-1, 1)[way])
        return pltpu.make_async_remote_copy(
            src_ref=gathered.at[block, core, q], dst_ref=gathered.at[block, core, q],
            send_sem=ag_s.at[way, hop - 1, q], recv_sem=ag_r.at[way, hop - 1, q],
            device_id=beside[way], device_id_type=MESH,
        )

    def share(step, q, half):
        block = at_z(step)
        return pltpu.make_async_remote_copy(
            src_ref=gathered.at[block, half, q], dst_ref=gathered.at[block, half, q],
            send_sem=pair_s.at[step + 3, q], recv_sem=pair_r.at[step + 3, q],
            device_id=partner, device_id_type=MESH,
        )

    loads[7].wait()

    def product(one, two, half, q):
        left = jnp.concatenate(
            [
                gathered[at_z(one), half, q].reshape(256, LANES),
                gathered[at_z(two), half, q].reshape(256, LANES),
            ],
            1,
        )
        right = jnp.concatenate([rec[at_z(one)], rec[at_z(two)]], 0)
        return jnp.dot(left, right, preferred_element_type=F32)

    def out_copies(half, q):
        rows = pl.ds(pl.multiple_of(half * 128 + q * 32, 32), 32)
        return [
            pltpu.make_async_copy(
                stage.at[:, rows, :], out.at[:, rows, :], out_sem.at[n, half, q]
            )
            for n, (stage, out) in enumerate(((stage_re, out_re), (stage_im, out_im)))
        ]

    def task(hop, half, q):
        if hop == 1:
            total[half, q] = product(-1, 1, half, q)
        elif hop < 4:
            total[half, q] += product(-hop, hop, half, q)
        else:
            stress = total[half, q] + product(0, 4, half, q)
            rows = pl.ds(pl.multiple_of(half * 128 + q * 32, 32), 32)
            for s in range(4):
                for n, stage in enumerate((stage_re, stage_im)):
                    stage[s, rows, :] = jnp.concatenate(
                        [stress[o * 64 + s * 16 + n * 8 :][:8] for o in range(4)], 0
                    ).astype(BF16)
            for copy in out_copies(half, q):
                copy.start()

    for q in range(CHUNKS):
        for o in range(4):
            source = q * 4 + o

            @pl.when(source != col)
            def _():
                back_copy(source, source).wait_recv()

        ag_copy(0, 1, q).start()
        ag_copy(1, 1, q).start()
        share(0, q, core).start()

    def shared_wait(hop, q):
        if hop < 4:
            share(-hop, q, other).wait_recv()
            share(hop, q, other).wait_recv()
        else:
            share(0, q, other).wait_recv()
            share(4, q, other).wait_recv()

    for hop in range(1, 4):

        def step(q, _, hop=hop, ways=(0, 1)):
            for way in range(2):
                ag_arrival(way, hop, q).wait_recv()
                if way in ways:
                    ag_copy(way, hop + 1, q).start()
                share(hop * (-1, 1)[way], q, core).start()
            task(hop, core, q)
            if hop > 1:
                shared_wait(hop - 1, q)
                task(hop - 1, other, q)
            return 0

        if hop < 3:
            lax.fori_loop(0, CHUNKS, step, 0)
        else:
            lax.fori_loop(0, 2, functools.partial(step, ways=(0,)), 0)
            lax.fori_loop(2, 4, functools.partial(step, ways=(1,)), 0)

    for way in range(2):

        def last(q, _, way=way):
            ag_arrival(way, 4, q).wait_recv()
            share(4, q, core).start()
            task(4, core, q)
            shared_wait(3, q)
            task(3, other, q)
            return 0

        lax.fori_loop(2 * way, 2 * way + 2, last, 0)

    def finish(q, _):
        shared_wait(4, q)
        task(4, other, q)
        return 0

    lax.fori_loop(0, CHUNKS, finish, 0)

    for copy in pair_copies.values():
        copy.wait_send()
    par_copy.wait_send()
    for way in range(2):
        for q in range(CHUNKS):
            for hop in range(4):
                if hop > 0 or q in longer[way]:
                    ring_copy(way, hop, q).wait_send()
                if hop < 3 or q in longer[way]:
                    ag_copy(way, hop + 1, q).wait_send()
    for n in range(COLS):

        @pl.when(n != col)
        def _():
            fwd_copy(n, col).wait_send()
            back_copy(n, col).wait_send()

    def ends(q, _):
        for step in range(-3, 5):
            share(step, q, core).wait_send()
        for half in range(2):
            for copy in out_copies(half, q):
                copy.wait()
        return 0

    lax.fori_loop(0, CHUNKS, ends, 0)


def local(pressure, basis, recovery, omega, damping, harmonic):
    fwd, inv = transforms()
    dma = pltpu.SemaphoreType.DMA
    anywhere = pl.BlockSpec(memory_space=pl.ANY)
    out = jax.ShapeDtypeStruct((4, 256, 1024), BF16)
    return pl.pallas_call(
        kernel,
        out_shape=(out, out),
        in_specs=[anywhere] * 8,
        out_specs=(anywhere, anywhere),
        scratch_shapes=[
            pltpu.VMEM((4, 256, 1024), BF16),
            pltpu.VMEM((1024, 1024), BF16),
            pltpu.VMEM((8, 128, 1024), BF16),
            pltpu.VMEM((33, 64), F32),
            pltpu.VMEM((33, 64), F32),
            pltpu.VMEM((1, 256), jnp.int32),
            pltpu.VMEM((512, 512), BF16),
            pltpu.VMEM((512, 512), BF16),
            pltpu.VMEM((8, CHUNKS, 128, LANES), F32),
            pltpu.VMEM((8, CHUNKS, 128, LANES), BF16),
            pltpu.VMEM((8, CHUNKS, 128, LANES), BF16),
            pltpu.VMEM((2, 40, LANES), F32),
            pltpu.VMEM((2, 40, LANES), F32),
            pltpu.VMEM((SECTORS, GROUP, LANES), F32),
            pltpu.VMEM((SECTORS, GROUP, LANES), F32),
            pltpu.VMEM((2, 4, CHUNKS, 128, LANES), BF16),
            pltpu.VMEM((2, 4, CHUNKS, 128, LANES), BF16),
            pltpu.VMEM((COLS, 2, 16, LANES), BF16),
            pltpu.VMEM((COLS, 2, 16, LANES), BF16),
            pltpu.VMEM((SECTORS, 16, LANES), BF16),
            pltpu.VMEM((8, 2, CHUNKS, 4, 4, 16, LANES), BF16),
            pltpu.VMEM((2, CHUNKS, 256, 1024), F32),
            pltpu.VMEM((4, 256, 1024), BF16),
            pltpu.VMEM((4, 256, 1024), BF16),
            dma((8,)),
            dma((8,)), dma((8,)),
            dma((2,)),
            dma((2, 4, CHUNKS)), dma((2, 4, CHUNKS)),
            dma((COLS,)), dma((COLS,)),
            dma((COLS,)), dma((COLS,)),
            dma((2, 4, CHUNKS)), dma((2, 4, CHUNKS)),
            dma((8, CHUNKS)), dma((8, CHUNKS)),
            dma((2, 2, CHUNKS)),
        ],
        compiler_params=pltpu.CompilerParams(
            collective_id=0, has_side_effects=True, vmem_limit_bytes=52 * 2**20
        ),
        cost_estimate=pl.CostEstimate(
            flops=7 * 2**30, bytes_accessed=12 * 2**20, transcendentals=0
        ),
    )(
        pressure, basis, recovery.reshape(8, 128, 1024), omega, damping,
        harmonic.reshape(1, 256), fwd, inv,
    )


def solution(mesh):
    in_specs = (
        P("sector", None, "mode"),
        P("mode", None),
        P(None, "mode"),
        P(None, "mode"),
        P(None, "mode"),
        P(),
    )
    out_specs = (P("sector", None, "mode"), P("sector", None, "mode"))
    return jax.shard_map(local, mesh=mesh, in_specs=in_specs, out_specs=out_specs, check_vma=False)
```

time: 172 us -> 72.3 us (0.42)
  waiting for transfers between devices: 109 us -> 0 us
  Pallas kernels: 0 us -> 62.6 us
  matrix products: 15.8 us -> 0 us
  between operations: 14.2 us -> 0.66 us
  blocking collectives: 10.3 us -> 0 us
  local copies, waits for them, and re-layouts: 15.8 us -> 8.76 us
  starting transfers between devices: 6.6 us -> 0 us
    pallas_call x0 -> x1, Pallas kernels: none -> 62.6 us  [local(): pl.pallas_call(kernel, out_shape=(out, out), in_specs=[anywhere] * 8, out...]
    reduce_scatter x1 -> x0, waiting for transfers between devices: 59.6 us -> none  [local(): lax.psum_scatter(lax.dot_general(basis, pressure_rows, (((0,), (1,)), (()...]
    all_gather x1 -> x0, waiting for transfers between devices: 43.3 us -> none  [local(): piece = lax.all_gather(in_sectors, 'mode', axis=0, tiled=True)]
    dot_general x8 -> x0, matrix products: 15.8 us -> none  [the longest x1 7.43 us: local(): lax.dot_general(piece.reshape(piece.shape[0], -1), recovery, (((0,), (0,)...]
    all_to_all x1 -> x0, blocking collectives: 10.3 us -> none  [local(): lax.all_to_all(responses, 'sector', split_axis=2, concat_axis=0, tiled=True)]
    reshape x2 -> x0, local copies, waits for them, and re-layouts: 9.41 us -> none  [the longest x1 7.78 us: local(): piece.reshape(piece.shape[0], -1)]
    all_to_all x1 -> x0, starting transfers between devices: 6.52 us -> none  [local(): lax.all_to_all(forces, 'sector', split_axis=0, concat_axis=1, tiled=True)]
    unnamed x10 -> x14, local copies, waits for them, and re-layouts: 2.37 us -> 8.76 us
  transfers between devices with their start and end apart: 3 -> 0, of which waited for: 3 -> 0; matrix products, arithmetic and copies ran while one was open for 0% -> 0% of each run, Pallas kernels for 0% -> 0%
where the time goes in v1:
time: 72.3 us; the launch traced here: 72 us
  Pallas kernels  62.6 us (87%)
  local copies, waits for them, and re-layouts  8.76 us (12%)
    pallas_call x1, Pallas kernels, local(): pl.pallas_call(kernel, out_shape=(out, out), in_specs=[anywhere] * 8, out...  62.6 us
    unnamed x14, local copies, waits for them, and re-layouts  8.76 us

profile of v1, /device:TPU:1, one launch (start us, length us, event | category | flops | bytes accessed | tf_op | source)
XLA Modules:
  0.0 72.0 jit_solution(9370052011412583787)
XLA Ops:
  0.6 0.0 copy-start
  0.6 0.7 copy-done
  1.4 0.0 copy-start.1
  1.4 0.7 %copy-done.1 = f32[33,64]{1,0:T(8,128)S(1)} copy-done((f32[33,64]{1,0:T(8,128)S(1)}, f32[33,64]{1,0:T(8,128)}, u32[]{:S(2)}) %copy-start.1) | copy-done | bytes 8472
  2.1 0.0 copy-start.2
  2.1 0.7 copy-done.2
  2.8 0.0 copy-start.3
  2.8 1.0 %copy-done.3 = bf16[512,512]{1,0:T(8,128)(2,1)S(1)} copy-done((bf16[512,512]{1,0:T(8,128)(2,1)S(1)}, bf16[512,512]{1,0:T(8,128)(2,1)}, u32[]{:S(2)}) %copy-start.3) | copy-done | bytes 524312
  3.8 0.0 copy-start.4
  3.8 1.0 %copy-done.4 = bf16[512,512]{1,0:T(8,128)(2,1)S(1)} copy-done((bf16[512,512]{1,0:T(8,128)(2,1)S(1)}, bf16[512,512]{1,0:T(8,128)(2,1)}, u32[]{:S(2)}) %copy-start.4) | copy-done | bytes 524312
  4.9 62.6 %shard_map.95 = (bf16[4,256,1024]{2,1,0:T(8,128)(2,1)}, bf16[4,256,1024]{2,1,0:T(8,128)(2,1)}) custom-call(bf16[4,256,1024]{2,1,0:T(8,128)(2,1)} %press_hbm.1, bf16[1024,1024]{1,0:T(8,128)(2,1)} %basis_hbm.1, bf16[8,128,1024]{2,1,0:T(8,128)(2,1)} %bitcast.3, f32[33,64]{1,0:T(8,128)S(1)} %copy-done, f32[33,64]{1,0:T(8,128)S(1)} %copy-done.1, ...), custom_call_target="tpu_custom_call" | custom-call | flops 7516192768 | bytes 12582912 | tf_op jit(solution)/shard_map/pallas_call | solution.py:405
  67.5 0.0 copy-start.5
  67.5 3.2 %copy.12 = bf16[4,256,1024]{2,1,0:T(8,128)(2,1)} copy(bf16[4,256,1024]{2,1,0:T(8,128)(2,1)} %get-tuple-element.4) | data formatting | bytes 4194304
  70.7 0.0 copy-done.5
  70.7 1.3 %copy.13 = bf16[4,256,1024]{2,1,0:T(8,128)(2,1)} copy(bf16[4,256,1024]{2,1,0:T(8,128)(2,1)S(1)} %copy-done.5) | data formatting | bytes 4194304
Async XLA Ops:
  0.6 0.7 %copy-start = (f32[33,64]{1,0:T(8,128)S(1)}, f32[33,64]{1,0:T(8,128)}, u32[]{:S(2)}) copy-start(f32[33,64]{1,0:T(8,128)} %omega_hbm.1) | copy-start | bytes 25348
  1.4 0.7 %copy-start.1 = (f32[33,64]{1,0:T(8,128)S(1)}, f32[33,64]{1,0:T(8,128)}, u32[]{:S(2)}) copy-start(f32[33,64]{1,0:T(8,128)} %damp_hbm.1) | copy-start | bytes 25348
  2.1 0.7 copy-start.2
  2.8 1.0 %copy-start.3 = (bf16[512,512]{1,0:T(8,128)(2,1)S(1)}, bf16[512,512]{1,0:T(8,128)(2,1)}, u32[]{:S(2)}) copy-start(bf16[512,512]{1,0:T(8,128)(2,1)} %constant.5.clone.inv_hbm) | copy-start | bytes 1572868
  3.8 1.0 %copy-start.4 = (bf16[512,512]{1,0:T(8,128)(2,1)S(1)}, bf16[512,512]{1,0:T(8,128)(2,1)}, u32[]{:S(2)}) copy-start(bf16[512,512]{1,0:T(8,128)(2,1)} %constant.4.clone.fwd_hbm) | copy-start | bytes 1572868
  67.5 3.2 %copy-start.5 = (bf16[4,256,1024]{2,1,0:T(8,128)(2,1)S(1)}, bf16[4,256,1024]{2,1,0:T(8,128)(2,1)}, u32[]{:S(2)}) copy-start(bf16[4,256,1024]{2,1,0:T(8,128)(2,1)} %get-tuple-element.5) | copy-start | bytes 6291460

commit v2 on v1

v2 whole, which is shorter than its diff:
```python
import functools
import math

import jax
import jax.numpy as jnp
from jax import lax
from jax.experimental import pallas as pl
from jax.experimental.pallas import tpu as pltpu
from jax.sharding import PartitionSpec as P

MESH = pl.DeviceIdType.MESH
SECTORS = 64
COLS = 16
LANES = 128
GROUP = 8
CHUNKS = 4
DIRECT = 2
F32 = jnp.float32
BF16 = jnp.bfloat16


def phase_values(diameter_dim):
    shape = (SECTORS, SECTORS)
    number = lax.broadcasted_iota(jnp.int32, shape, diameter_dim)
    sector = lax.broadcasted_iota(jnp.int32, shape, 1 - diameter_dim)
    half = SECTORS // 2
    sine = number > half
    diameter = jnp.where(sine, number - half, number)
    angle = (2.0 * math.pi / SECTORS) * ((diameter * sector) % SECTORS).astype(F32)
    value = jnp.where(sine, -jnp.sin(angle), jnp.cos(angle))
    once = (number == 0) | (number == half)
    return value, jnp.where(once, 1.0 / SECTORS, 2.0 / SECTORS)


def per_sample(table):
    size = SECTORS * GROUP
    rows = jnp.broadcast_to(table[:, None, :], (SECTORS, GROUP, SECTORS)).reshape(size, SECTORS)
    spread = (
        lax.broadcasted_iota(jnp.int32, (SECTORS, size), 0)
        == lax.broadcasted_iota(jnp.int32, (SECTORS, size), 1) // GROUP
    )
    wide = jnp.dot(
        rows.astype(BF16), spread.astype(F32).astype(BF16), preferred_element_type=F32
    )
    same = (
        lax.broadcasted_iota(jnp.int32, (size, size), 0) % GROUP
        == lax.broadcasted_iota(jnp.int32, (size, size), 1) % GROUP
    )
    return jnp.where(same, wide, 0.0).astype(BF16)


def kernel(
    press_hbm, basis_hbm, rec_hbm, omega_hbm, damp_hbm, harm_hbm,
    stage_re, stage_im,
    press, basis, rec, omega, damp, harm, fwd, inv,
    own, give, take, params, params_in, recv_re, recv_im,
    ring_out, ring_in, loads_out, loads_in, resp_out, gathered, total,
    load_sem, give_s, give_r, par_sem, ring_s, ring_r, fwd_s, fwd_r, back_s, back_r,
    ag_s, ag_r, pair_s, pair_r, ready,
):
    col = lax.axis_index("sector")
    place = lax.axis_index("mode")
    z = place // 2
    core = place % 2
    other = 1 - core
    y = col // 4
    partner = (col, z * 2 + other)

    def at_z(step):
        return (z + step + 8) % 8

    up = (col, at_z(1) * 2 + core)
    down = (col, at_z(-1) * 2 + core)
    beside = (up, down)

    def samples(half):
        return pl.ds(pl.multiple_of(half * 128, 128), 128)

    load_press = [
        pltpu.make_async_copy(
            press_hbm.at[:, samples(half), :], press.at[:, samples(half), :], load_sem.at[n]
        )
        for n, half in enumerate((other, core))
    ]
    def load_basis(n):
        columns = pl.ds(n * 256 if isinstance(n, int) else pl.multiple_of(n * 256, 256), 256)
        return pltpu.make_async_copy(
            basis_hbm.at[:, columns], basis.at[:, columns], load_sem.at[2 + n]
        )

    load_small = [
        pltpu.make_async_copy(a, b, load_sem.at[6 + n])
        for n, (a, b) in enumerate(((omega_hbm, omega), (damp_hbm, damp), (harm_hbm, harm)))
    ]
    load_rec = pltpu.make_async_copy(rec_hbm, rec, load_sem.at[9])
    load_press[0].start()
    for n in range(4):
        load_basis(n).start()
    load_press[1].start()
    for copy in load_small:
        copy.start()

    barrier = pltpu.get_barrier_semaphore()
    for device in (up, down, partner):
        pl.semaphore_signal(barrier, inc=1, device_id=device, device_id_type=MESH)
    for step in range(1, COLS):
        pl.semaphore_signal(
            barrier, inc=1, device_id=((col + step) % COLS, place), device_id_type=MESH
        )

    def partial(half, target, n):
        part = jnp.dot(
            press[:, samples(half), :].reshape(512, 1024),
            basis[:, pl.ds(pl.multiple_of(n * 256, 256), 256)],
            preferred_element_type=F32,
        ).astype(target.dtype)
        for b in range(2):
            for q in range(CHUNKS):
                for s in range(4):
                    target[2 * n + b, q, s * 32 : s * 32 + 32, :] = part[
                        s * 128 + q * 32 : s * 128 + q * 32 + 32, b * 128 : b * 128 + 128
                    ]

    def give_tile(n, _):
        load_basis(n).wait()
        partial(other, give, n)
        return 0

    def own_tile(n, _):
        partial(core, own, (z // 2 + 2 + n) % 4)
        return 0

    load_press[0].wait()
    lax.fori_loop(0, 4, give_tile, 0)
    load_press[1].wait()
    pl.semaphore_wait(barrier, COLS + 2)

    def pair_copy(n, block):
        return pltpu.make_async_remote_copy(
            src_ref=give.at[block], dst_ref=take.at[block], send_sem=give_s.at[n],
            recv_sem=give_r.at[n], device_id=partner, device_id_type=MESH,
        )

    order = (4, 3, -3, 2, -2, 1, -1, 0)
    pair_copies = {}
    for n, step in enumerate(order):
        pair_copies[step] = pair_copy(n, at_z(step))
        pair_copies[step].start()
    for step in range(1, COLS):
        pl.semaphore_signal(
            ready, inc=1, device_id=((col + step) % COLS, place), device_id_type=MESH
        )
    load_rec.start()

    longer = ((0, 2), (1, 3))
    shorter = ((1, 3), (0, 2))

    def ring_copy(way, hop, q):
        return pltpu.make_async_remote_copy(
            src_ref=ring_out.at[way, hop, q], dst_ref=ring_in.at[way, hop, q],
            send_sem=ring_s.at[way, hop, q], recv_sem=ring_r.at[way, hop, q],
            device_id=beside[way], device_id_type=MESH,
        )

    def pair_sum(block, q):
        return own[block, q] + take[block, q].astype(F32)

    def ring_sum(way, hop, q):
        value = pair_sum(at_z((4 - hop) * (1, -1)[way]), q)
        if hop > 1 or (hop == 1 and q in longer[way]):
            ring_copy(way, hop - 1, q).wait_recv()
            value = value + ring_in[way, hop - 1, q].astype(F32)
        return value

    def ring_steps(hop, chunks):
        for n in range(2):
            for way in range(2):
                q = chunks[way][n]
                ring_out[way, hop, q] = ring_sum(way, hop, q).astype(BF16)
                ring_copy(way, hop, q).start()

    planes = (place, at_z(1) * 2 + core, at_z(-1) * 2 + core)

    def fwd_copy(kind, to, source):
        return pltpu.make_async_remote_copy(
            src_ref=loads_out.at[kind, to], dst_ref=loads_in.at[kind, source],
            send_sem=fwd_s.at[kind, to], recv_sem=fwd_r.at[kind, source],
            device_id=(to, planes[kind]), device_id_type=MESH,
        )

    def send_loads(kind, q, force):
        for o in range(4):
            to = q * 4 + o
            for pair in range(2):
                at = 2 * pair * 32 + o * 8
                loads_out[kind, to, pair] = jnp.concatenate(
                    [force[at : at + 8], force[at + 32 : at + 40]], 0
                ).astype(BF16)
            if kind:
                fwd_copy(kind, to, col).start()
            else:

                @pl.when(to != col)
                def _():
                    fwd_copy(0, to, col).start()

                @pl.when(to == col)
                def _():
                    loads_in[0, col] = loads_out[0, col]

    lax.fori_loop(0, 1, own_tile, 0)
    pair_copies[4].wait_recv()
    ring_steps(0, longer)
    lax.fori_loop(1, 4, own_tile, 0)
    for step in (3, -3):
        pair_copies[step].wait_recv()
    ring_steps(1, shorter)
    for step in (2, -2, 1, -1, 0):
        pair_copies[step].wait_recv()
    for q in range(CHUNKS):
        send_loads(0, q, pair_sum(z, q))

    for copy in load_small:
        copy.wait()
    params[...] = jnp.zeros_like(params)
    for n, ref in enumerate((omega, damp)):
        mine = ref[...]
        none = jnp.zeros_like(mine)
        params[n, 0:33, :] = jnp.concatenate(
            [jnp.where(core == 0, mine, none), jnp.where(core == 1, mine, none)], 1
        )

    par_copy = pltpu.make_async_remote_copy(
        src_ref=params, dst_ref=params_in, send_sem=par_sem.at[0], recv_sem=par_sem.at[1],
        device_id=partner, device_id_type=MESH,
    )
    par_copy.start()

    ring_steps(1, longer)

    forward, _ = phase_values(0)
    fwd[...] = per_sample(forward)
    backward, weight = phase_values(1)
    inv[...] = per_sample(backward * weight)

    ring_steps(2, shorter)
    ring_steps(2, longer)

    par_copy.wait_recv()
    both = params[...] + params_in[...]
    freq = both[0, 0:33, :][:, None, :]
    ratio = both[1, 0:33, :][:, None, :]
    sample = lax.broadcasted_iota(jnp.int32, (GROUP, 256), 0)
    lane = lax.broadcasted_iota(jnp.int32, (GROUP, 256), 1)
    here = lane == core * 128 + col * GROUP + sample
    picked = jnp.where(here, harm[...].astype(F32), 0.0)
    drive = (0.25 * jnp.sum(picked, axis=1, keepdims=True))[None, :, :]
    stiff = freq * freq - drive * drive
    loss = 2.0 * ratio * freq * drive
    size = stiff * stiff + loss * loss
    for ref, value in ((recv_re, stiff / size), (recv_im, -loss / size)):
        ref[0:33] = value
        ref[33:64] = value[1:32]

    pl.semaphore_wait(ready, COLS - 1)
    for chunks in (shorter, longer):
        for n in range(2):
            for way in range(2):
                q = chunks[way][n]
                send_loads(way + 1, q, ring_sum(way, 3, q))

    for source in range(COLS):
        fwd_copy(1, source, source).wait_recv()
        fwd_copy(2, source, source).wait_recv()

        @pl.when(source != col)
        def _():
            fwd_copy(0, source, source).wait_recv()

    force = (
        loads_in[0].astype(F32) + loads_in[1].astype(F32) + loads_in[2].astype(F32)
    ).astype(BF16).reshape(512, LANES)
    wave = jnp.dot(fwd[...], force, preferred_element_type=F32)
    response = jnp.concatenate(
        [
            (wave * recv_re[...].reshape(512, LANES)).astype(BF16),
            (wave * recv_im[...].reshape(512, LANES)).astype(BF16),
        ],
        1,
    )
    back = jnp.dot(inv[...], response, preferred_element_type=F32)
    resp_out[...] = jnp.concatenate(
        [
            back[:, :LANES].reshape(SECTORS, GROUP, LANES),
            back[:, LANES:].reshape(SECTORS, GROUP, LANES),
        ],
        1,
    ).astype(BF16)

    def back_copy(kind, to, source):
        return pltpu.make_async_remote_copy(
            src_ref=resp_out.at[pl.ds(to * 4, 4)],
            dst_ref=gathered.at[z, core, source // 4, source % 4],
            send_sem=back_s.at[kind, to], recv_sem=back_r.at[kind, source],
            device_id=(to, planes[kind]), device_id_type=MESH,
        )

    for step in (10, 9, 11, 6, 14, 5, 7, 13, 15, 2, 8, 1, 3, 4, 12, 0):
        to = (col + step) % COLS

        @pl.when(y < DIRECT)
        def _():
            back_copy(1, to, col).start()
            back_copy(2, to, col).start()

        if step:
            back_copy(0, to, col).start()
    gathered[z, core, y, col % 4] = resp_out[pl.ds(col * 4, 4)]

    def back_arrival(kind, source):
        block = at_z((0, -1, 1)[kind])
        return pltpu.make_async_remote_copy(
            src_ref=resp_out.at[pl.ds(source * 4, 4)],
            dst_ref=gathered.at[block, core, source // 4, source % 4],
            send_sem=back_s.at[kind, source], recv_sem=back_r.at[kind, source],
            device_id=(source, planes[kind]), device_id_type=MESH,
        )

    def ag_copy(way, hop, q):
        block = at_z((1 - hop) * (1, -1)[way])
        return pltpu.make_async_remote_copy(
            src_ref=gathered.at[block, core, q], dst_ref=gathered.at[block, core, q],
            send_sem=ag_s.at[way, hop - 1, q], recv_sem=ag_r.at[way, hop - 1, q],
            device_id=beside[way], device_id_type=MESH,
        )

    def ag_arrival(way, hop, q):
        block = at_z(hop * (-1, 1)[way])
        return pltpu.make_async_remote_copy(
            src_ref=gathered.at[block, core, q], dst_ref=gathered.at[block, core, q],
            send_sem=ag_s.at[way, hop - 1, q], recv_sem=ag_r.at[way, hop - 1, q],
            device_id=beside[way], device_id_type=MESH,
        )

    def share(step, q, half):
        block = at_z(step)
        return pltpu.make_async_remote_copy(
            src_ref=gathered.at[block, half, q], dst_ref=gathered.at[block, half, q],
            send_sem=pair_s.at[step + 3, q], recv_sem=pair_r.at[step + 3, q],
            device_id=partner, device_id_type=MESH,
        )

    load_rec.wait()

    def task(hop, half, q):
        one, two = (at_z(-hop), at_z(hop)) if hop < 4 else (at_z(0), at_z(4))
        rows = pl.ds(pl.multiple_of(half * 128 + q * 32, 32), 32)

        left = jnp.concatenate([gathered[b, half, q].reshape(256, LANES) for b in (one, two)], 1)
        right = jnp.concatenate([rec[b] for b in (one, two)], 0)
        part = jnp.dot(left, right, preferred_element_type=F32)
        if hop == 1:
            total[half, q] = part
        elif hop < 4:
            total[half, q] += part
        else:
            stress = total[half, q] + part
            for s in range(4):
                for n, stage in enumerate((stage_re, stage_im)):
                    stage[s, rows, :] = jnp.concatenate(
                        [stress[o * 64 + s * 16 + n * 8 :][:8] for o in range(4)], 0
                    ).astype(BF16)

    def begin(q):
        for o in range(4):
            source = q * 4 + o

            @pl.when(source != col)
            def _():
                back_arrival(0, source).wait_recv()

        if q >= DIRECT:
            ag_copy(0, 1, q).start()
            ag_copy(1, 1, q).start()
        share(0, q, core).start()

    def arrive(hop, q):
        for way in range(2):
            if hop < 4 or q in longer[way]:
                if hop == 1 and q < DIRECT:
                    for o in range(4):
                        back_arrival(way + 1, q * 4 + o).wait_recv()
                else:
                    ag_arrival(way, hop, q).wait_recv()
                if hop < 3 or (hop == 3 and q in longer[way]):
                    ag_copy(way, hop + 1, q).start()
                share(hop * (-1, 1)[way] if hop < 4 else 4, q, core).start()

    def shared_task(hop, q):
        for step in (-hop, hop) if hop < 4 else (0, 4):
            share(step, q, other).wait_recv()
        task(hop, other, q)

    begin(2)
    begin(3)
    pending = None
    for hop, q in (
        (1, 0), (1, 1), (0, 0), (0, 1), (1, 2), (1, 3), (2, 0), (2, 1), (2, 2), (2, 3),
        (3, 0), (3, 1), (3, 2), (3, 3), (4, 0), (4, 1), (4, 2), (4, 3),
    ):
        if hop == 0:
            begin(q)
            continue
        arrive(hop, q)
        task(hop, core, q)
        if pending is not None:
            shared_task(*pending)
        pending = (hop, q)
    shared_task(*pending)

    for copy in pair_copies.values():
        copy.wait_send()
    par_copy.wait_send()
    for way in range(2):
        for q in range(CHUNKS):
            for hop in range(4):
                if hop < 3 and (hop > 0 or q in longer[way]):
                    ring_copy(way, hop, q).wait_send()
                if (hop > 0 or q >= DIRECT) and (hop < 3 or q in longer[way]):
                    ag_copy(way, hop + 1, q).wait_send()
    for n in range(COLS):
        for kind in (1, 2):
            fwd_copy(kind, n, col).wait_send()

            @pl.when(y < DIRECT)
            def _():
                back_copy(kind, n, col).wait_send()

        @pl.when(n != col)
        def _():
            fwd_copy(0, n, col).wait_send()
            back_copy(0, n, col).wait_send()

    def ends(q, _):
        for step in range(-3, 5):
            share(step, q, core).wait_send()
        return 0

    lax.fori_loop(0, CHUNKS, ends, 0)


def write_out(stage_re, stage_im, out_re, out_im, sem):
    copies = [
        pltpu.make_async_copy(stage.at[s], out.at[s], sem.at[n, s])
        for n, (stage, out) in enumerate(((stage_re, out_re), (stage_im, out_im)))
        for s in range(4)
    ]
    for copy in copies:
        copy.start()
    for copy in copies:
        copy.wait()


def local(pressure, basis, recovery, omega, damping, harmonic):
    dma = pltpu.SemaphoreType.DMA
    anywhere = pl.BlockSpec(memory_space=pl.ANY)
    held = pl.BlockSpec(memory_space=pltpu.VMEM)
    out = jax.ShapeDtypeStruct((4, 256, 1024), BF16)
    stage = pltpu.VMEM((4, 256, 1024), BF16)
    staged = pl.pallas_call(
        kernel,
        out_shape=(stage, stage),
        in_specs=[anywhere] * 6,
        out_specs=(held, held),
        scratch_shapes=[
            pltpu.VMEM((4, 256, 1024), BF16),
            pltpu.VMEM((1024, 1024), BF16),
            pltpu.VMEM((8, 128, 1024), BF16),
            pltpu.VMEM((33, 64), F32),
            pltpu.VMEM((33, 64), F32),
            pltpu.VMEM((1, 256), jnp.int32),
            pltpu.VMEM((512, 512), BF16),
            pltpu.VMEM((512, 512), BF16),
            pltpu.VMEM((8, CHUNKS, 128, LANES), F32),
            pltpu.VMEM((8, CHUNKS, 128, LANES), BF16),
            pltpu.VMEM((8, CHUNKS, 128, LANES), BF16),
            pltpu.VMEM((2, 40, LANES), F32),
            pltpu.VMEM((2, 40, LANES), F32),
            pltpu.VMEM((SECTORS, GROUP, LANES), F32),
            pltpu.VMEM((SECTORS, GROUP, LANES), F32),
            pltpu.VMEM((2, 4, CHUNKS, 128, LANES), BF16),
            pltpu.VMEM((2, 4, CHUNKS, 128, LANES), BF16),
            pltpu.VMEM((3, COLS, 2, 16, LANES), BF16),
            pltpu.VMEM((3, COLS, 2, 16, LANES), BF16),
            pltpu.VMEM((SECTORS, 16, LANES), BF16),
            pltpu.VMEM((8, 2, CHUNKS, 4, 4, 16, LANES), BF16),
            pltpu.VMEM((2, CHUNKS, 256, 1024), F32),
            dma((10,)),
            dma((8,)), dma((8,)),
            dma((2,)),
            dma((2, 4, CHUNKS)), dma((2, 4, CHUNKS)),
            dma((3, COLS)), dma((3, COLS)),
            dma((3, COLS)), dma((3, COLS)),
            dma((2, 4, CHUNKS)), dma((2, 4, CHUNKS)),
            dma((8, CHUNKS)), dma((8, CHUNKS)),
            pltpu.SemaphoreType.REGULAR,
        ],
        compiler_params=pltpu.CompilerParams(
            collective_id=0, has_side_effects=True, vmem_limit_bytes=52 * 2**20
        ),
        cost_estimate=pl.CostEstimate(
            flops=7 * 2**30, bytes_accessed=12 * 2**20, transcendentals=0
        ),
    )(
        *(
            pltpu.with_memory_space_constraint(array, pltpu.HBM)
            for array in (
                pressure, basis, recovery.reshape(8, 128, 1024), omega, damping,
                harmonic.reshape(1, 256),
            )
        )
    )
    return pl.pallas_call(
        write_out,
        out_shape=(out, out),
        in_specs=[anywhere, anywhere],
        out_specs=(anywhere, anywhere),
        scratch_shapes=[dma((2, 4))],
        compiler_params=pltpu.CompilerParams(vmem_limit_bytes=2**20),
    )(*(pltpu.with_memory_space_constraint(array, pltpu.VMEM) for array in staged))


def solution(mesh):
    in_specs = (
        P("sector", None, "mode"),
        P("mode", None),
        P(None, "mode"),
        P(None, "mode"),
        P(None, "mode"),
        P(),
    )
    out_specs = (P("sector", None, "mode"), P("sector", None, "mode"))
    return jax.shard_map(local, mesh=mesh, in_specs=in_specs, out_specs=out_specs, check_vma=False)
```

time: 72.3 us -> 61.2 us (0.85)
  local copies, waits for them, and re-layouts: 8.76 us -> 0 us
  Pallas kernels: 62.6 us -> 60.4 us
    unnamed x14 -> x0, local copies, waits for them, and re-layouts: 8.76 us -> none
    pallas_call x1 -> x2, Pallas kernels: 62.6 us -> 60.4 us  [the longest x1 58.4 us: local(): pl.pallas_call(kernel, out_shape=(stage, stage), in_specs=[anywhere] * 6,...]
where the time goes in v2:
time: 61.2 us; the launch traced here: 61.1 us
  Pallas kernels  60.4 us (99%)
  between operations  0.64 us (1%)
    pallas_call x1, Pallas kernels, local(): pl.pallas_call(kernel, out_shape=(stage, stage), in_specs=[anywhere] * 6,...  58.4 us
    pallas_call x1, Pallas kernels, local(): pl.pallas_call(write_out, out_shape=(out, out), in_specs=[anywhere, anywh...  2.07 us

profile of v2, /device:TPU:1, one launch (start us, length us, event | category | flops | bytes accessed | tf_op | source)
XLA Modules:
  0.0 61.1 jit_solution(14172055092103601212)
XLA Ops:
  0.6 58.4 %shard_map.77 = (bf16[4,256,1024]{2,1,0:T(8,128)(2,1)S(1)}, bf16[4,256,1024]{2,1,0:T(8,128)(2,1)S(1)}) custom-call(bf16[4,256,1024]{2,1,0:T(8,128)(2,1)} %press_hbm.1, bf16[1024,1024]{1,0:T(8,128)(2,1)} %basis_hbm.1, bf16[8,128,1024]{2,1,0:T(8,128)(2,1)} %bitcast.2, f32[33,64]{1,0:T(8,128)} %omega_hbm.1, f32[33,64]{1,0:T(8,128)} %damp_hbm.1, s32[1,256]{1,0:T(1,128)} %bitcast.3), custom_call_target="tpu_custom_call" | custom-call | flops 7516192768 | bytes 12582912 | tf_op jit(solution)/shard_map/pallas_call | solution.py:470
  59.0 2.1 %shard_map.78 = (bf16[4,256,1024]{2,1,0:T(8,128)(2,1)}, bf16[4,256,1024]{2,1,0:T(8,128)(2,1)}) custom-call(bf16[4,256,1024]{2,1,0:T(8,128)(2,1)S(1)} %get-tuple-element.4.stage_re, bf16[4,256,1024]{2,1,0:T(8,128)(2,1)S(1)} %get-tuple-element.5.stage_im), custom_call_target="tpu_custom_call" | custom-call | tf_op jit(solution)/shard_map/pallas_call | solution.py:523

commit v3 on v2

--- a/solution.py
+++ b/solution.py
@@ -135,9 +135,21 @@
     load_press[1].wait()
     pl.semaphore_wait(barrier, COLS + 2)
 
+    def all_sent(ref, sem):
+        pltpu.make_async_remote_copy(
+            src_ref=ref, dst_ref=ref, send_sem=sem, recv_sem=sem,
+            device_id=partner, device_id_type=MESH,
+        ).wait_send()
+
+    def all_arrived(ref, sem):
+        pltpu.make_async_remote_copy(
+            src_ref=ref, dst_ref=ref, send_sem=sem, recv_sem=sem,
+            device_id=partner, device_id_type=MESH,
+        ).wait_recv()
+
     def pair_copy(n, block):
         return pltpu.make_async_remote_copy(
-            src_ref=give.at[block], dst_ref=take.at[block], send_sem=give_s.at[n],
+            src_ref=give.at[block], dst_ref=take.at[block], send_sem=give_s.at[0],
             recv_sem=give_r.at[n], device_id=partner, device_id_type=MESH,
         )
 
@@ -155,10 +167,14 @@
     longer = ((0, 2), (1, 3))
     shorter = ((1, 3), (0, 2))
 
+    def ring_slot(way, hop, q):
+        return way * 10 + (longer[way].index(q) if hop == 0 else hop * 4 - 2 + q)
+
     def ring_copy(way, hop, q):
-        return pltpu.make_async_remote_copy(
-            src_ref=ring_out.at[way, hop, q], dst_ref=ring_in.at[way, hop, q],
-            send_sem=ring_s.at[way, hop, q], recv_sem=ring_r.at[way, hop, q],
+        slot = ring_slot(way, hop, q)
+        return pltpu.make_async_remote_copy(
+            src_ref=ring_out.at[slot], dst_ref=ring_in.at[slot],
+            send_sem=ring_s.at[0], recv_sem=ring_r.at[slot],
             device_id=beside[way], device_id_type=MESH,
         )
 
@@ -169,14 +185,14 @@
         value = pair_sum(at_z((4 - hop) * (1, -1)[way]), q)
         if hop > 1 or (hop == 1 and q in longer[way]):
             ring_copy(way, hop - 1, q).wait_recv()
-            value = value + ring_in[way, hop - 1, q].astype(F32)
+            value = value + ring_in[ring_slot(way, hop - 1, q)].astype(F32)
         return value
 
     def ring_steps(hop, chunks):
         for n in range(2):
             for way in range(2):
                 q = chunks[way][n]
-                ring_out[way, hop, q] = ring_sum(way, hop, q).astype(BF16)
+                ring_out[ring_slot(way, hop, q)] = ring_sum(way, hop, q).astype(BF16)
                 ring_copy(way, hop, q).start()
 
     planes = (place, at_z(1) * 2 + core, at_z(-1) * 2 + core)
@@ -184,7 +200,7 @@
     def fwd_copy(kind, to, source):
         return pltpu.make_async_remote_copy(
             src_ref=loads_out.at[kind, to], dst_ref=loads_in.at[kind, source],
-            send_sem=fwd_s.at[kind, to], recv_sem=fwd_r.at[kind, source],
+            send_sem=fwd_s.at[kind], recv_sem=fwd_r.at[kind],
             device_id=(to, planes[kind]), device_id_type=MESH,
         )
 
@@ -269,13 +285,9 @@
                 q = chunks[way][n]
                 send_loads(way + 1, q, ring_sum(way, 3, q))
 
-    for source in range(COLS):
-        fwd_copy(1, source, source).wait_recv()
-        fwd_copy(2, source, source).wait_recv()
-
-        @pl.when(source != col)
-        def _():
-            fwd_copy(0, source, source).wait_recv()
+    all_arrived(loads_in.at[0, pl.ds(0, COLS - 1)], fwd_r.at[0])
+    all_arrived(loads_in.at[1], fwd_r.at[1])
+    all_arrived(loads_in.at[2], fwd_r.at[2])
 
     force = (
         loads_in[0].astype(F32) + loads_in[1].astype(F32) + loads_in[2].astype(F32)
@@ -301,7 +313,7 @@
         return pltpu.make_async_remote_copy(
             src_ref=resp_out.at[pl.ds(to * 4, 4)],
             dst_ref=gathered.at[z, core, source // 4, source % 4],
-            send_sem=back_s.at[kind, to], recv_sem=back_r.at[kind, source],
+            send_sem=back_s.at[kind], recv_sem=back_r.at[kind, source // 4],
             device_id=(to, planes[kind]), device_id_type=MESH,
         )
 
@@ -317,20 +329,25 @@
             back_copy(0, to, col).start()
     gathered[z, core, y, col % 4] = resp_out[pl.ds(col * 4, 4)]
 
-    def back_arrival(kind, source):
+    def back_arrival(kind, q, count=4):
         block = at_z((0, -1, 1)[kind])
-        return pltpu.make_async_remote_copy(
-            src_ref=resp_out.at[pl.ds(source * 4, 4)],
-            dst_ref=gathered.at[block, core, source // 4, source % 4],
-            send_sem=back_s.at[kind, source], recv_sem=back_r.at[kind, source],
-            device_id=(source, planes[kind]), device_id_type=MESH,
-        )
+        all_arrived(gathered.at[block, core, q, pl.ds(0, count)], back_r.at[kind, q])
+
+    def ag_slot(way, hop, q):
+        first = 4 - DIRECT
+        if hop == 1:
+            slot = q - DIRECT
+        elif hop < 4:
+            slot = first + (hop - 2) * 4 + q
+        else:
+            slot = first + 8 + longer[way].index(q)
+        return way * (first + 10) + slot
 
     def ag_copy(way, hop, q):
         block = at_z((1 - hop) * (1, -1)[way])
         return pltpu.make_async_remote_copy(
             src_ref=gathered.at[block, core, q], dst_ref=gathered.at[block, core, q],
-            send_sem=ag_s.at[way, hop - 1, q], recv_sem=ag_r.at[way, hop - 1, q],
+            send_sem=ag_s.at[0], recv_sem=ag_r.at[ag_slot(way, hop, q)],
             device_id=beside[way], device_id_type=MESH,
         )
 
@@ -338,7 +355,7 @@
         block = at_z(hop * (-1, 1)[way])
         return pltpu.make_async_remote_copy(
             src_ref=gathered.at[block, core, q], dst_ref=gathered.at[block, core, q],
-            send_sem=ag_s.at[way, hop - 1, q], recv_sem=ag_r.at[way, hop - 1, q],
+            send_sem=ag_s.at[0], recv_sem=ag_r.at[ag_slot(way, hop, q)],
             device_id=beside[way], device_id_type=MESH,
         )
 
@@ -346,7 +363,7 @@
         block = at_z(step)
         return pltpu.make_async_remote_copy(
             src_ref=gathered.at[block, half, q], dst_ref=gathered.at[block, half, q],
-            send_sem=pair_s.at[step + 3, q], recv_sem=pair_r.at[step + 3, q],
+            send_sem=pair_s.at[0], recv_sem=pair_r.at[(abs(step) + 3) % 4, q],
             device_id=partner, device_id_type=MESH,
         )
 
@@ -372,12 +389,13 @@
                     ).astype(BF16)
 
     def begin(q):
-        for o in range(4):
-            source = q * 4 + o
-
-            @pl.when(source != col)
-            def _():
-                back_arrival(0, source).wait_recv()
+        @pl.when(y == q)
+        def _():
+            back_arrival(0, q, 3)
+
+        @pl.when(y != q)
+        def _():
+            back_arrival(0, q)
 
         if q >= DIRECT:
             ag_copy(0, 1, q).start()
@@ -388,8 +406,7 @@
         for way in range(2):
             if hop < 4 or q in longer[way]:
                 if hop == 1 and q < DIRECT:
-                    for o in range(4):
-                        back_arrival(way + 1, q * 4 + o).wait_recv()
+                    back_arrival(way + 1, q)
                 else:
                     ag_arrival(way, hop, q).wait_recv()
                 if hop < 3 or (hop == 3 and q in longer[way]):
@@ -397,8 +414,7 @@
                 share(hop * (-1, 1)[way] if hop < 4 else 4, q, core).start()
 
     def shared_task(hop, q):
-        for step in (-hop, hop) if hop < 4 else (0, 4):
-            share(step, q, other).wait_recv()
+        all_arrived(gathered.at[pl.ds(0, 2), other, q], pair_r.at[hop - 1, q])
         task(hop, other, q)
 
     begin(2)
@@ -418,35 +434,20 @@
         pending = (hop, q)
     shared_task(*pending)
 
-    for copy in pair_copies.values():
-        copy.wait_send()
+    all_sent(give, give_s.at[0])
     par_copy.wait_send()
-    for way in range(2):
-        for q in range(CHUNKS):
-            for hop in range(4):
-                if hop < 3 and (hop > 0 or q in longer[way]):
-                    ring_copy(way, hop, q).wait_send()
-                if (hop > 0 or q >= DIRECT) and (hop < 3 or q in longer[way]):
-                    ag_copy(way, hop + 1, q).wait_send()
-    for n in range(COLS):
-        for kind in (1, 2):
-            fwd_copy(kind, n, col).wait_send()
-
-            @pl.when(y < DIRECT)
-            def _():
-                back_copy(kind, n, col).wait_send()
-
-        @pl.when(n != col)
+    all_sent(ring_out, ring_s.at[0])
+    all_sent(loads_out.at[0, pl.ds(0, COLS - 1)], fwd_s.at[0])
+    all_sent(resp_out.at[pl.ds(0, 4 * (COLS - 1))], back_s.at[0])
+    for kind in (1, 2):
+        all_sent(loads_out.at[kind], fwd_s.at[kind])
+
+        @pl.when(y < DIRECT)
         def _():
-            fwd_copy(0, n, col).wait_send()
-            back_copy(0, n, col).wait_send()
-
-    def ends(q, _):
-        for step in range(-3, 5):
-            share(step, q, core).wait_send()
-        return 0
-
-    lax.fori_loop(0, CHUNKS, ends, 0)
+            all_sent(resp_out, back_s.at[kind])
+
+    all_sent(gathered.at[pl.ds(0, 4)], pair_s.at[0])
+    all_sent(gathered.at[pl.ds(0, 7 - DIRECT // 2), 0], ag_s.at[0])
 
 
 def write_out(stage_re, stage_im, out_re, out_im, sem):
@@ -488,21 +489,21 @@
             pltpu.VMEM((2, 40, LANES), F32),
             pltpu.VMEM((SECTORS, GROUP, LANES), F32),
             pltpu.VMEM((SECTORS, GROUP, LANES), F32),
-            pltpu.VMEM((2, 4, CHUNKS, 128, LANES), BF16),
-            pltpu.VMEM((2, 4, CHUNKS, 128, LANES), BF16),
+            pltpu.VMEM((20, 128, LANES), BF16),
+            pltpu.VMEM((20, 128, LANES), BF16),
             pltpu.VMEM((3, COLS, 2, 16, LANES), BF16),
             pltpu.VMEM((3, COLS, 2, 16, LANES), BF16),
             pltpu.VMEM((SECTORS, 16, LANES), BF16),
             pltpu.VMEM((8, 2, CHUNKS, 4, 4, 16, LANES), BF16),
             pltpu.VMEM((2, CHUNKS, 256, 1024), F32),
             dma((10,)),
-            dma((8,)), dma((8,)),
+            dma((1,)), dma((8,)),
             dma((2,)),
-            dma((2, 4, CHUNKS)), dma((2, 4, CHUNKS)),
-            dma((3, COLS)), dma((3, COLS)),
-            dma((3, COLS)), dma((3, COLS)),
-            dma((2, 4, CHUNKS)), dma((2, 4, CHUNKS)),
-            dma((8, CHUNKS)), dma((8, CHUNKS)),
+            dma((1,)), dma((20,)),
+            dma((3,)), dma((3,)),
+            dma((3,)), dma((3, CHUNKS)),
+            dma((1,)), dma((2 * (14 - DIRECT),)),
+            dma((1,)), dma((4, CHUNKS)),
             pltpu.SemaphoreType.REGULAR,
         ],
         compiler_params=pltpu.CompilerParams(

time: 61.2 us -> 58.2 us (0.951)
  Pallas kernels: 60.4 us -> 57.5 us
    pallas_call x1, Pallas kernels: 58.4 us -> 55.4 us  [local(): pl.pallas_call(kernel, out_shape=(stage, stage), in_specs=[anywhere] * 6,...]
where the time goes in v3:
time: 58.2 us; the launch traced here: 58.1 us
  Pallas kernels  57.5 us (99%)
  between operations  0.64 us (1%)
    pallas_call x1, Pallas kernels, local(): pl.pallas_call(kernel, out_shape=(stage, stage), in_specs=[anywhere] * 6,...  55.4 us
    pallas_call x1, Pallas kernels, local(): pl.pallas_call(write_out, out_shape=(out, out), in_specs=[anywhere, anywh...  2.07 us

profile of v3, /device:TPU:1, one launch (start us, length us, event | category | flops | bytes accessed | tf_op | source)
XLA Modules:
  0.0 58.1 jit_solution(11829962577277113003)
XLA Ops:
  0.6 55.4 %shard_map.77 = (bf16[4,256,1024]{2,1,0:T(8,128)(2,1)S(1)}, bf16[4,256,1024]{2,1,0:T(8,128)(2,1)S(1)}) custom-call(bf16[4,256,1024]{2,1,0:T(8,128)(2,1)} %press_hbm.1, bf16[1024,1024]{1,0:T(8,128)(2,1)} %basis_hbm.1, bf16[8,128,1024]{2,1,0:T(8,128)(2,1)} %bitcast.2, f32[33,64]{1,0:T(8,128)} %omega_hbm.1, f32[33,64]{1,0:T(8,128)} %damp_hbm.1, s32[1,256]{1,0:T(1,128)} %bitcast.3), custom_call_target="tpu_custom_call" | custom-call | flops 7516192768 | bytes 12582912 | tf_op jit(solution)/shard_map/pallas_call | solution.py:471
  56.1 2.1 %shard_map.78 = (bf16[4,256,1024]{2,1,0:T(8,128)(2,1)}, bf16[4,256,1024]{2,1,0:T(8,128)(2,1)}) custom-call(bf16[4,256,1024]{2,1,0:T(8,128)(2,1)S(1)} %get-tuple-element.4.stage_re, bf16[4,256,1024]{2,1,0:T(8,128)(2,1)S(1)} %get-tuple-element.5.stage_im), custom_call_target="tpu_custom_call" | custom-call | tf_op jit(solution)/shard_map/pallas_call | solution.py:524

commit v4 on v3

--- a/solution.py
+++ b/solution.py
@@ -15,6 +15,7 @@
 GROUP = 8
 CHUNKS = 4
 DIRECT = 2
+LATER = (2, 3)
 F32 = jnp.float32
 BF16 = jnp.bfloat16
 
@@ -51,7 +52,7 @@
 
 def kernel(
     press_hbm, basis_hbm, rec_hbm, omega_hbm, damp_hbm, harm_hbm,
-    stage_re, stage_im,
+    stage_re, stage_im, rest, last_left, last_right,
     press, basis, rec, omega, damp, harm, fwd, inv,
     own, give, take, params, params_in, recv_re, recv_im,
     ring_out, ring_in, loads_out, loads_in, resp_out, gathered, total,
@@ -157,7 +158,8 @@
     pair_copies = {}
     for n, step in enumerate(order):
         pair_copies[step] = pair_copy(n, at_z(step))
-        pair_copies[step].start()
+    pair_copies[4].start()
+
     for step in range(1, COLS):
         pl.semaphore_signal(
             ready, inc=1, device_id=((col + step) % COLS, place), device_id_type=MESH
@@ -225,6 +227,8 @@
                     loads_in[0, col] = loads_out[0, col]
 
     lax.fori_loop(0, 1, own_tile, 0)
+    for step in order[1:]:
+        pair_copies[step].start()
     pair_copies[4].wait_recv()
     ring_steps(0, longer)
     lax.fori_loop(1, 4, own_tile, 0)
@@ -369,24 +373,33 @@
 
     load_rec.wait()
 
+    def blocks(one, two, half, q):
+        return jnp.concatenate([gathered[b, half, q].reshape(256, LANES) for b in (one, two)], 1)
+
+    last_right[0:LANES, :] = rec[z]
+    last_right[LANES:, :] = rec[at_z(4)]
+
     def task(hop, half, q):
-        one, two = (at_z(-hop), at_z(hop)) if hop < 4 else (at_z(0), at_z(4))
-        rows = pl.ds(pl.multiple_of(half * 128 + q * 32, 32), 32)
-
-        left = jnp.concatenate([gathered[b, half, q].reshape(256, LANES) for b in (one, two)], 1)
-        right = jnp.concatenate([rec[b] for b in (one, two)], 0)
-        part = jnp.dot(left, right, preferred_element_type=F32)
+        if hop == 4 and q in LATER:
+            last_left[half, q - LATER[0]] = blocks(z, at_z(4), half, q)
+            return
+        if hop == 4:
+            part = jnp.dot(
+                blocks(z, at_z(4), half, q), last_right[...], preferred_element_type=F32
+            )
+            put_stress(total[half, q] + part, stage_re, stage_im, half, q)
+            return
+        one, two = at_z(-hop), at_z(hop)
+        part = jnp.dot(
+            blocks(one, two, half, q),
+            jnp.concatenate([rec[b] for b in (one, two)], 0),
+            preferred_element_type=F32,
+        )
+        target, row = (rest, q - LATER[0]) if q in LATER else (total, q)
         if hop == 1:
-            total[half, q] = part
-        elif hop < 4:
-            total[half, q] += part
+            target[half, row] = part
         else:
-            stress = total[half, q] + part
-            for s in range(4):
-                for n, stage in enumerate((stage_re, stage_im)):
-                    stage[s, rows, :] = jnp.concatenate(
-                        [stress[o * 64 + s * 16 + n * 8 :][:8] for o in range(4)], 0
-                    ).astype(BF16)
+            target[half, row] += part
 
     def begin(q):
         @pl.when(y == q)
@@ -450,14 +463,45 @@
     all_sent(gathered.at[pl.ds(0, 7 - DIRECT // 2), 0], ag_s.at[0])
 
 
-def write_out(stage_re, stage_im, out_re, out_im, sem):
+def put_stress(stress, stage_re, stage_im, half, place):
+    start = half * (stage_re.shape[1] // 2) + place * 32
+    if not isinstance(start, int):
+        start = pl.multiple_of(start, 32)
+    rows = pl.ds(start, 32)
+    for s in range(4):
+        for n, stage in enumerate((stage_re, stage_im)):
+            stage[s, rows, :] = jnp.concatenate(
+                [stress[o * 64 + s * 16 + n * 8 :][:8] for o in range(4)], 0
+            ).astype(BF16)
+
+
+def write_out(
+    stage_re, stage_im, rest, last_left, last_right, out_re, out_im, late_re, late_im, sem
+):
+    early = 32 * LATER[0]
     copies = [
-        pltpu.make_async_copy(stage.at[s], out.at[s], sem.at[n, s])
+        pltpu.make_async_copy(
+            stage.at[:, pl.ds(half * early, early), :],
+            out.at[:, pl.ds(half * 128, early), :],
+            sem.at[n, half, 0],
+        )
         for n, (stage, out) in enumerate(((stage_re, out_re), (stage_im, out_im)))
-        for s in range(4)
+        for half in range(2)
     ]
     for copy in copies:
         copy.start()
+    for half in range(2):
+        for row, q in enumerate(LATER):
+            part = jnp.dot(last_left[half, row], last_right[...], preferred_element_type=F32)
+            put_stress(rest[half, row] + part, late_re, late_im, half, row)
+            for n, (stage, out) in enumerate(((late_re, out_re), (late_im, out_im))):
+                copy = pltpu.make_async_copy(
+                    stage.at[:, pl.ds(half * 32 * len(LATER) + row * 32, 32), :],
+                    out.at[:, pl.ds(half * 128 + q * 32, 32), :],
+                    sem.at[n, half, 1 + row],
+                )
+                copy.start()
+                copies.append(copy)
     for copy in copies:
         copy.wait()
 
@@ -467,12 +511,18 @@
     anywhere = pl.BlockSpec(memory_space=pl.ANY)
     held = pl.BlockSpec(memory_space=pltpu.VMEM)
     out = jax.ShapeDtypeStruct((4, 256, 1024), BF16)
-    stage = pltpu.VMEM((4, 256, 1024), BF16)
+    early, late = 64 * LATER[0], 64 * len(LATER)
+    stage = pltpu.VMEM((4, early, 1024), BF16)
     staged = pl.pallas_call(
         kernel,
-        out_shape=(stage, stage),
+        out_shape=(
+            stage, stage,
+            pltpu.VMEM((2, len(LATER), 256, 1024), F32),
+            pltpu.VMEM((2, len(LATER), 256, 2 * LANES), BF16),
+            pltpu.VMEM((2 * LANES, 1024), BF16),
+        ),
         in_specs=[anywhere] * 6,
-        out_specs=(held, held),
+        out_specs=(held,) * 5,
         scratch_shapes=[
             pltpu.VMEM((4, 256, 1024), BF16),
             pltpu.VMEM((1024, 1024), BF16),
@@ -495,7 +545,7 @@
             pltpu.VMEM((3, COLS, 2, 16, LANES), BF16),
             pltpu.VMEM((SECTORS, 16, LANES), BF16),
             pltpu.VMEM((8, 2, CHUNKS, 4, 4, 16, LANES), BF16),
-            pltpu.VMEM((2, CHUNKS, 256, 1024), F32),
+            pltpu.VMEM((2, LATER[0], 256, 1024), F32),
             dma((10,)),
             dma((1,)), dma((8,)),
             dma((2,)),
@@ -524,10 +574,13 @@
     return pl.pallas_call(
         write_out,
         out_shape=(out, out),
-        in_specs=[anywhere, anywhere],
+        in_specs=[held] * 5,
         out_specs=(anywhere, anywhere),
-        scratch_shapes=[dma((2, 4))],
-        compiler_params=pltpu.CompilerParams(vmem_limit_bytes=2**20),
+        scratch_shapes=[
+            pltpu.VMEM((4, late, 1024), BF16), pltpu.VMEM((4, late, 1024), BF16),
+            dma((2, 2, 1 + len(LATER))),
+        ],
+        compiler_params=pltpu.CompilerParams(vmem_limit_bytes=8 * 2**20),
     )(*(pltpu.with_memory_space_constraint(array, pltpu.VMEM) for array in staged))
 
 

time: 58.2 us -> 57.7 us (level)
  no operation moved by 1% of the time
where the time goes in v4:
time: 57.7 us; the launch traced here: 57.6 us
  Pallas kernels  57 us (99%)
  between operations  0.64 us (1%)
    pallas_call x1, Pallas kernels, local(): pl.pallas_call(kernel, out_shape=(stage, stage, pltpu.VMEM((2, len(LATER)...  54.9 us
    pallas_call x1, Pallas kernels, local(): pl.pallas_call(write_out, out_shape=(out, out), in_specs=[held] * 5, out_...  2.12 us

profile of v4, /device:TPU:1, one launch (start us, length us, event | category | flops | bytes accessed | tf_op | source)
XLA Modules:
  0.0 57.6 jit_solution(13328520889795226706)
XLA Ops:
  0.6 54.9 %shard_map.77 = (bf16[4,128,1024]{2,1,0:T(8,128)(2,1)S(1)}, bf16[4,128,1024]{2,1,0:T(8,128)(2,1)S(1)}, f32[2,2,256,1024]{3,2,1,0:T(8,128)S(1)}, bf16[2,2,256,256...) custom-call(bf16[4,256,1024]{2,1,0:T(8,128)(2,1)} %press_hbm.1, bf16[1024,1024]{1,0:T(8,128)(2,1)} %basis_hbm.1, ...), custom_call_target="tpu_custom_call" | custom-call | flops 7516192768 | bytes 12582912 | tf_op jit(solution)/shard_map/pallas_call | solution.py:516
  55.5 2.1 %shard_map.78 = (bf16[4,256,1024]{2,1,0:T(8,128)(2,1)}, bf16[4,256,1024]{2,1,0:T(8,128)(2,1)}) custom-call(bf16[4,128,1024]{2,1,0:T(8,128)(2,1)S(1)} %get-tuple-element.7.stage_re, bf16[4,128,1024]{2,1,0:T(8,128)(2,1)S(1)} %get-tuple-element.8.stage_im, f32[2,2,256,1024]{3,2,1,0:T(8,128)S(1)} %get-tuple-element.9.rest, ...), custom_call_target="tpu_custom_call" | custom-call | tf_op jit(solution)/shard_map/pallas_call | solution.py:574

commit v5 on v4

--- a/solution.py
+++ b/solution.py
@@ -57,7 +57,7 @@
     own, give, take, params, params_in, recv_re, recv_im,
     ring_out, ring_in, loads_out, loads_in, resp_out, gathered, total,
     load_sem, give_s, give_r, par_sem, ring_s, ring_r, fwd_s, fwd_r, back_s, back_r,
-    ag_s, ag_r, pair_s, pair_r, ready,
+    ag_s, ag_r, pair_r, ready,
 ):
     col = lax.axis_index("sector")
     place = lax.axis_index("mode")
@@ -151,7 +151,7 @@
     def pair_copy(n, block):
         return pltpu.make_async_remote_copy(
             src_ref=give.at[block], dst_ref=take.at[block], send_sem=give_s.at[0],
-            recv_sem=give_r.at[n], device_id=partner, device_id_type=MESH,
+            recv_sem=give_r.at[(n + 1) // 2 if n < 3 else 2], device_id=partner, device_id_type=MESH,
         )
 
     order = (4, 3, -3, 2, -2, 1, -1, 0)
@@ -229,14 +229,12 @@
     lax.fori_loop(0, 1, own_tile, 0)
     for step in order[1:]:
         pair_copies[step].start()
-    pair_copies[4].wait_recv()
+    all_arrived(take.at[0], give_r.at[0])
     ring_steps(0, longer)
     lax.fori_loop(1, 4, own_tile, 0)
-    for step in (3, -3):
-        pair_copies[step].wait_recv()
+    all_arrived(take.at[pl.ds(0, 2)], give_r.at[1])
     ring_steps(1, shorter)
-    for step in (2, -2, 1, -1, 0):
-        pair_copies[step].wait_recv()
+    all_arrived(take.at[pl.ds(0, 5)], give_r.at[2])
     for q in range(CHUNKS):
         send_loads(0, q, pair_sum(z, q))
 
@@ -304,38 +302,40 @@
         ],
         1,
     )
-    back = jnp.dot(inv[...], response, preferred_element_type=F32)
-    resp_out[...] = jnp.concatenate(
-        [
-            back[:, :LANES].reshape(SECTORS, GROUP, LANES),
-            back[:, LANES:].reshape(SECTORS, GROUP, LANES),
-        ],
-        1,
-    ).astype(BF16)
-
     def back_copy(kind, to, source):
         return pltpu.make_async_remote_copy(
             src_ref=resp_out.at[pl.ds(to * 4, 4)],
             dst_ref=gathered.at[z, core, source // 4, source % 4],
-            send_sem=back_s.at[kind], recv_sem=back_r.at[kind, source // 4],
+            send_sem=back_s.at[kind], recv_sem=back_r.at[(0, 4, 6)[kind] + source // 4],
             device_id=(to, planes[kind]), device_id_type=MESH,
         )
 
-    for step in (10, 9, 11, 6, 14, 5, 7, 13, 15, 2, 8, 1, 3, 4, 12, 0):
-        to = (col + step) % COLS
-
-        @pl.when(y < DIRECT)
-        def _():
-            back_copy(1, to, col).start()
-            back_copy(2, to, col).start()
-
-        if step:
-            back_copy(0, to, col).start()
+    for half in range(2):
+        back = jnp.dot(inv[half * 256 : half * 256 + 256], response, preferred_element_type=F32)
+        resp_out[half * 32 : half * 32 + 32] = jnp.concatenate(
+            [
+                back[:, :LANES].reshape(SECTORS // 2, GROUP, LANES),
+                back[:, LANES:].reshape(SECTORS // 2, GROUP, LANES),
+            ],
+            1,
+        ).astype(BF16)
+        for step in (5, 2, 6, 1, 7, 3, 4, 0):
+            to = half * 8 + (col + step) % 8
+
+            @pl.when(y < DIRECT)
+            def _():
+                back_copy(1, to, col).start()
+                back_copy(2, to, col).start()
+
+            @pl.when(to != col)
+            def _():
+                back_copy(0, to, col).start()
+
     gathered[z, core, y, col % 4] = resp_out[pl.ds(col * 4, 4)]
 
     def back_arrival(kind, q, count=4):
         block = at_z((0, -1, 1)[kind])
-        all_arrived(gathered.at[block, core, q, pl.ds(0, count)], back_r.at[kind, q])
+        all_arrived(gathered.at[block, core, q, pl.ds(0, count)], back_r.at[(0, 4, 6)[kind] + q])
 
     def ag_slot(way, hop, q):
         first = 4 - DIRECT
@@ -367,7 +367,7 @@
         block = at_z(step)
         return pltpu.make_async_remote_copy(
             src_ref=gathered.at[block, half, q], dst_ref=gathered.at[block, half, q],
-            send_sem=pair_s.at[0], recv_sem=pair_r.at[(abs(step) + 3) % 4, q],
+            send_sem=ag_s.at[0], recv_sem=pair_r.at[(abs(step) + 3) % 4, q],
             device_id=partner, device_id_type=MESH,
         )
 
@@ -459,8 +459,7 @@
         def _():
             all_sent(resp_out, back_s.at[kind])
 
-    all_sent(gathered.at[pl.ds(0, 4)], pair_s.at[0])
-    all_sent(gathered.at[pl.ds(0, 7 - DIRECT // 2), 0], ag_s.at[0])
+    all_sent(gathered.at[pl.ds(0, 7)], ag_s.at[0])
 
 
 def put_stress(stress, stage_re, stage_im, half, place):
@@ -547,13 +546,13 @@
             pltpu.VMEM((8, 2, CHUNKS, 4, 4, 16, LANES), BF16),
             pltpu.VMEM((2, LATER[0], 256, 1024), F32),
             dma((10,)),
-            dma((1,)), dma((8,)),
+            dma((1,)), dma((3,)),
             dma((2,)),
             dma((1,)), dma((20,)),
             dma((3,)), dma((3,)),
-            dma((3,)), dma((3, CHUNKS)),
+            dma((3,)), dma((8,)),
             dma((1,)), dma((2 * (14 - DIRECT),)),
-            dma((1,)), dma((4, CHUNKS)),
+            dma((4, CHUNKS)),
             pltpu.SemaphoreType.REGULAR,
         ],
         compiler_params=pltpu.CompilerParams(

time: 57.7 us -> 57.5 us (level)
  no operation moved by 1% of the time
where the time goes in v5:
time: 57.5 us; the launch traced here: 57.4 us
  Pallas kernels  56.8 us (99%)
  between operations  0.64 us (1%)
    pallas_call x1, Pallas kernels, local(): pl.pallas_call(kernel, out_shape=(stage, stage, pltpu.VMEM((2, len(LATER)...  54.7 us
    pallas_call x1, Pallas kernels, local(): pl.pallas_call(write_out, out_shape=(out, out), in_specs=[held] * 5, out_...  2.12 us

profile of v5, /device:TPU:1, one launch (start us, length us, event | category | flops | bytes accessed | tf_op | source)
XLA Modules:
  0.0 57.4 jit_solution(13785943292540125336)
XLA Ops:
  0.6 54.7 %shard_map.77 = (bf16[4,128,1024]{2,1,0:T(8,128)(2,1)S(1)}, bf16[4,128,1024]{2,1,0:T(8,128)(2,1)S(1)}, f32[2,2,256,1024]{3,2,1,0:T(8,128)S(1)}, bf16[2,2,256,256...) custom-call(bf16[4,256,1024]{2,1,0:T(8,128)(2,1)} %press_hbm.1, bf16[1024,1024]{1,0:T(8,128)(2,1)} %basis_hbm.1, ...), custom_call_target="tpu_custom_call" | custom-call | flops 7516192768 | bytes 12582912 | tf_op jit(solution)/shard_map/pallas_call | solution.py:515
  55.3 2.1 %shard_map.78 = (bf16[4,256,1024]{2,1,0:T(8,128)(2,1)}, bf16[4,256,1024]{2,1,0:T(8,128)(2,1)}) custom-call(bf16[4,128,1024]{2,1,0:T(8,128)(2,1)S(1)} %get-tuple-element.7.stage_re, bf16[4,128,1024]{2,1,0:T(8,128)(2,1)S(1)} %get-tuple-element.8.stage_im, f32[2,2,256,1024]{3,2,1,0:T(8,128)S(1)} %get-tuple-element.9.rest, ...), custom_call_target="tpu_custom_call" | custom-call | tf_op jit(solution)/shard_map/pallas_call | solution.py:573
